TPU v7x, 1024 devices: a whole 4x4x32 slice. The times are simulated.
1024 devices in a mesh: dp: 32 (over z_lo, x), mp: 32 (over z_hi, y, core).
Axes of the slice: x: 4, y: 4, z: 32 (z_hi: 4, z_lo: 8; z = z_hi * 8 + z_lo), core: 2. Of those that a mesh axis runs over, the one named last changes fastest.
Arguments:
- patches: bfloat16 [4096, 6144], P('dp', 'mp'), may hold values from -6 to 6
- route_owner: int32 [4096], P('dp'), may hold values from 0 to 31, as said below
- route_slot: int32 [4096], P('dp'), may hold values from 0 to 127, as said below
- segment_ids: int32 [32, 128], P('dp'), may hold values from 0 to 3, never falling along the last dimension, each value on 1 to 64 neighbouring positions
- ln_gain: float32 [6144], replicated, may hold values from 0.25 to 1.75
- qkv_weight: bfloat16 [6144, 12288], P(None, 'mp'), may hold values from -0.078125 to 0.078125
- q_gain: float32 [4096], P('mp'), may hold values from 0.25 to 1.75
- k_gain: float32 [4096], P('mp'), may hold values from 0.25 to 1.75
- d_attn: bfloat16 [4096, 4096], P('dp', 'mp'), may hold values from -6 to 6
Outputs:
- attn_out: bfloat16 [4096, 4096], P('dp', 'mp')
- norm_grad: float32 [6144, 4096], P('mp', 'dp')
- weight_grad: float32 [6144, 12288], P('dp', 'mp')
Inputs may be any that keep to these rules, and one draw needn't show every extreme that they name: `route_owner`: of the rows of one device of dp, at most 12 have one owner, and on every draw some device sends exactly 12 rows to some owner and some owner receives exactly 12 from some device; every owner receives exactly 128 rows in all. `route_slot`: together with route_owner, every position of every owner's sequence is named by exactly one row.
All inputs are finite; a program needn't handle non-finite values.
Results may differ from a plain program's by a relative error of at most 0.03.
Values may be sent and summed in bfloat16 or wider, within the bound.
A program may use at most 32 MiB of HBM per device.

v0:
```python
import math

import jax
import jax.numpy as jnp
from jax import lax
from jax.sharding import PartitionSpec as P

D = 6144
HEAD = 128
CAP = 12


def norm_head(vector, gain_row):
    center = vector - jnp.mean(vector, axis=-1, keepdims=True)
    inverse = lax.rsqrt(jnp.mean(center * center, axis=-1, keepdims=True) + 1e-06)
    unit_rows = center * inverse
    return (unit_rows * gain_row, unit_rows, inverse)


def norm_head_back(cotangent, unit_rows, inverse, gain_row):
    scaled = cotangent * gain_row
    return inverse * (
        scaled
        - jnp.mean(scaled, axis=-1, keepdims=True)
        - unit_rows * jnp.mean(scaled * unit_rows, axis=-1, keepdims=True)
    )


def head_pass(block, gain_query, gain_key, segments, cotangent):
    size_head = block.shape[1] // 3
    query_raw = block[:, :size_head].astype(jnp.float32)
    key_raw = block[:, size_head : 2 * size_head].astype(jnp.float32)
    value_rows = block[:, 2 * size_head :]
    query_n, query_u, query_r = norm_head(query_raw, gain_query)
    key_n, key_u, key_r = norm_head(key_raw, gain_key)
    factor = 1.0 / math.sqrt(size_head)
    scores = jnp.dot(query_n, key_n.T, precision=lax.Precision.HIGHEST) * factor
    allowed = segments[:, None] == segments[None, :]
    scores = jnp.where(allowed, scores, -1e30)
    shifted = jnp.exp(scores - jnp.max(scores, axis=1, keepdims=True))
    softmax_rows = shifted / jnp.sum(shifted, axis=1, keepdims=True)
    probs_low = softmax_rows.astype(jnp.bfloat16)
    attended = jnp.dot(probs_low, value_rows, preferred_element_type=jnp.float32).astype(
        jnp.bfloat16
    )
    grad_value = jnp.dot(probs_low.T, cotangent, preferred_element_type=jnp.float32)
    grad_probs = jnp.dot(cotangent, value_rows.T, preferred_element_type=jnp.float32)
    grad_scores = softmax_rows * (
        grad_probs - jnp.sum(grad_probs * softmax_rows, axis=1, keepdims=True)
    )
    grad_qn = jnp.dot(grad_scores, key_n, precision=lax.Precision.HIGHEST) * factor
    grad_kn = jnp.dot(grad_scores.T, query_n, precision=lax.Precision.HIGHEST) * factor
    grad_query = norm_head_back(grad_qn, query_u, query_r, gain_query)
    grad_key = norm_head_back(grad_kn, key_u, key_r, gain_key)
    joined = jnp.concatenate([grad_query, grad_key, grad_value], axis=1)
    return (attended, joined.astype(jnp.bfloat16))


def on_device(
    patches, route_owner, route_slot, segment_ids, ln_gain, qkv_weight, q_gain, k_gain, d_attn
):
    owners = lax.axis_size("dp")
    row_count, shard_width = patches.shape
    owner_ids = jnp.arange(owners)
    dest_hot = (route_owner[:, None] == owner_ids[None, :]).astype(jnp.int32)
    earlier = jnp.cumsum(dest_hot, axis=0) - dest_hot
    dest_rank = jnp.sum(earlier * dest_hot, axis=1)
    target = route_owner * CAP + dest_rank
    send_pick = jnp.arange(owners * CAP)[:, None] == target[None, :]
    outgoing = jnp.dot(
        send_pick.astype(jnp.bfloat16), patches, preferred_element_type=jnp.float32
    ).astype(jnp.bfloat16)
    slot_out = jnp.sum(jnp.where(send_pick, route_slot[None, :] + 1, 0), axis=1) - 1
    arrived, slot_in = (
        lax.all_to_all(
            outgoing.reshape(owners, CAP, shard_width),
            "dp",
            split_axis=0,
            concat_axis=0,
            tiled=True,
        ),
        lax.all_to_all(
            slot_out.reshape(owners, CAP), "dp", split_axis=0, concat_axis=0, tiled=True
        ),
    )
    placing = (jnp.arange(row_count)[:, None] == slot_in.reshape(1, owners * CAP)).astype(
        jnp.bfloat16
    )
    local_rows = jnp.dot(
        placing, arrived.reshape(owners * CAP, shard_width), preferred_element_type=jnp.float32
    ).astype(jnp.bfloat16)
    values = local_rows.astype(jnp.float32)
    row_total, squares = lax.psum((jnp.sum(values, axis=1), jnp.sum(values * values, axis=1)), "mp")
    row_mean = row_total / D
    inverse = lax.rsqrt(squares / D - row_mean * row_mean + 1e-06)
    gain_shard = lax.dynamic_slice_in_dim(ln_gain, lax.axis_index("mp") * shard_width, shard_width)
    normed = ((values - row_mean[:, None]) * inverse[:, None] * gain_shard[None, :]).astype(
        jnp.bfloat16
    )
    gathered = lax.all_gather(normed, "mp", axis=1, tiled=True)
    projected = jnp.dot(gathered, qkv_weight, preferred_element_type=jnp.float32).astype(
        jnp.bfloat16
    )
    local_heads = qkv_weight.shape[1] // (3 * HEAD)
    blocks = projected.reshape(row_count, local_heads, 3 * HEAD).transpose(1, 0, 2)
    cot_heads = d_attn.reshape(row_count, local_heads, HEAD).transpose(1, 0, 2)
    attended, grads = jax.vmap(head_pass, in_axes=(0, 0, 0, None, 0))(
        blocks,
        q_gain.reshape(local_heads, HEAD),
        k_gain.reshape(local_heads, HEAD),
        segment_ids[0],
        cot_heads,
    )
    attn_out = attended.transpose(1, 0, 2).reshape(row_count, local_heads * HEAD)
    grads = grads.transpose(1, 0, 2).reshape(row_count, local_heads * 3 * HEAD)
    norm_grad = lax.psum_scatter(
        lax.dot_general(
            qkv_weight, grads, (((1,), (1,)), ((), ())), preferred_element_type=jnp.float32
        ).astype(jnp.bfloat16),
        "mp",
        scatter_dimension=0,
        tiled=True,
    ).astype(jnp.float32)
    partial_w = lax.dot_general(
        gathered, grads, (((0,), (0,)), ((), ())), preferred_element_type=jnp.float32
    )
    weight_grad = lax.psum_scatter(
        partial_w.astype(jnp.bfloat16), "dp", scatter_dimension=0, tiled=True
    ).astype(jnp.float32)
    return (attn_out, norm_grad, weight_grad)


def solution(mesh):
    in_specs = (
        P("dp", "mp"),
        P("dp"),
        P("dp"),
        P("dp", None),
        P(),
        P(None, "mp"),
        P("mp"),
        P("mp"),
        P("dp", "mp"),
    )
    out_specs = (P("dp", "mp"), P("mp", "dp"), P("dp", "mp"))
    return jax.shard_map(
        on_device, mesh=mesh, in_specs=in_specs, out_specs=out_specs, check_vma=False
    )
```

profile of v0, /device:TPU:24, one launch (start us, length us, event | category | flops | bytes accessed | tf_op | source)
XLA Modules:
  0.0 740.1 jit_solution(8586656269400781637)
XLA Ops:
  7.2 0.7 fusion.32
  8.1 0.8 select_reduce_fusion.1
  8.9 0.7 multiply_add_fusion
  9.8 0.7 sub.84
  10.5 15.4 %all-to-all-start = ((s32[32,1,12]{2,1,0:T(1,128)}), s32[32,1,12]{2,1,0:T(1,128)S(1)}, u32[]{:S(2)}, u32[]{:S(2)}) async-start(s32[32,1,12]{2,1,0:T(1,128)} %bitcast.1), calls=%async_computation | async-start | bytes 32768 | tf_op jit(solution)/shard_map/all_to_all | solution.py:82
  26.2 0.8 reshape.204
  27.0 11.4 %all-to-all-done = s32[32,1,12]{2,1,0:T(1,128)S(1)} async-done(((s32[32,1,12]{2,1,0:T(1,128)}), s32[32,1,12]{2,1,0:T(1,128)S(1)}, u32[]{:S(2)}, u32[]{:S(2)}) %all-to-all-start) | async-done | bytes 1568 | tf_op jit(solution)/shard_map/all_to_all | solution.py:82
  38.4 3.9 all-to-all-start.1
  42.3 0.8 dynamic_slice.3
  43.1 0.5 broadcast.145
  43.6 0.7 reduce.19
  44.4 16.0 %all-to-all-done.1 = bf16[32,12,192]{2,1,0:T(8,128)(2,1)S(1)} async-done(((bf16[32,12,192]{2,1,0:T(8,128)(2,1)}), bf16[32,12,192]{2,1,0:T(8,128)(2,1)S(1)}, u32[]{:S(2)}, u32[]{:S(2)}) %all-to-all-start.1) | async-done | bytes 147488 | tf_op jit(solution)/shard_map/all_to_all | solution.py:75
  60.5 0.3 fusion.61
  60.7 122.6 %all-reduce = (f32[128]{0:T(128)S(1)}, f32[128]{0:T(128)S(1)}) all-reduce(f32[128]{0:T(128)S(1)} %get-tuple-element.22, f32[128]{0:T(128)S(1)} %get-tuple-element.21), channel_id=1, replica_groups=mesh['dp'=32,'mp'=32] {'mp'}, use_global_device_ids=true, to_apply=%region_6.7 | all-reduce | flops 256 | bytes 2048 | tf_op jit(solution)/shard_map/psum | solution.py:93
  183.4 0.7 multiply_convert_fusion
  184.2 0.7 broadcast_multiply_fusion.1
  184.8 0.7 broadcast_multiply_fusion
  185.5 120.9 %all-gather.2.cloned.1.call-done = bf16[128,6144]{0,1:T(8,128)(2,1)} async-done(((bf16[128,192]{0,1:T(8,128)(2,1)}), bf16[128,6144]{0,1:T(8,128)(2,1)}) %all-gather.2.cloned.1.call-update) | async-done | bytes 1572880 | tf_op jit(solution)/shard_map/all_gather | solution.py:100
  306.3 3.8 fusion.1
  310.6 0.3 fusion.62
  311.3 0.4 fusion.63
  311.7 0.4 fusion.27
  312.2 0.2 fusion.35
  312.4 3.9 fusion
  316.4 1.6 copy.36
  318.1 3.5 convolution_convert_fusion
  321.6 0.8 convolution_convert_fusion.6
  322.4 156.4 %reduce-scatter.7.cloned.1.call-done = bf16[192,128]{1,0:T(8,128)(2,1)} async-done(((bf16[6144,128]{1,0:T(8,128)(2,1)}), bf16[192,128]{1,0:T(8,128)(2,1)}) %reduce-scatter.7.cloned.1.call-update) | async-done | bytes 49168
  478.8 0.9 copy.37
  479.7 0.7 copy.32
  480.5 251.5 %reduce-scatter.5.cloned.1.call-done = bf16[192,384]{1,0:T(8,128)(2,1)} async-done(((bf16[6144,384]{1,0:T(8,128)(2,1)}), bf16[192,384]{1,0:T(8,128)(2,1)}) %reduce-scatter.5.cloned.1.call-update) | async-done | bytes 147472 | tf_op jit(solution)/shard_map/reduce_scatter | solution.py:127
  732.0 1.6 convert_element_type.67
  (40 shorter events, 1.8 us)
Async XLA Ops:
  7.2 18.7 %copy-start = (bf16[128,192]{0,1:T(8,128)(2,1)S(1)}, bf16[128,192]{0,1:T(8,128)(2,1)}, u32[]{:S(2)}) copy-start(bf16[128,192]{0,1:T(8,128)(2,1)} %param.9) | copy-start | bytes 147460
  10.5 27.9 %all-to-all-start = ((s32[32,1,12]{2,1,0:T(1,128)}), s32[32,1,12]{2,1,0:T(1,128)S(1)}, u32[]{:S(2)}, u32[]{:S(2)}) async-start(s32[32,1,12]{2,1,0:T(1,128)} %bitcast.1), calls=%async_computation | async-start | bytes 32768 | tf_op jit(solution)/shard_map/all_to_all | solution.py:82
  38.4 22.0 %all-to-all-start.1 = ((bf16[32,12,192]{2,1,0:T(8,128)(2,1)}), bf16[32,12,192]{2,1,0:T(8,128)(2,1)S(1)}, u32[]{:S(2)}, u32[]{:S(2)}) async-start(bf16[32,12,192]{2,1,0:T(8,128)(2,1)} %reshape.204), calls=%async_computation.1 | async-start | bytes 524288 | tf_op jit(solution)/shard_map/all_to_all | solution.py:75
  42.3 264.1 %all-gather.2.cloned.1.call-start = ((), (), s32[]{:S(2)}) async-start(), calls=%async_computation.4 | async-start | bytes 1622016 | tf_op jit(solution)/shard_map/all_gather | solution.py:100
  184.1 294.7 %reduce-scatter.7.cloned.1.call-start = ((), (), s32[]{:S(2)}) async-start(), calls=%async_computation.6 | async-start | bytes 1622016
  185.5 125.0 %copy-start.3 = (s32[1,128]{1,0:T(1,128)S(1)}, s32[1,128]{1,0:T(1,128)}, u32[]{:S(2)}) copy-start(s32[1,128]{1,0:T(1,128)} %param.12) | copy-start | bytes 1540
  185.5 125.1 %copy-start.4 = (f32[128]{0:T(128)S(1)}, f32[128]{0:T(128)}, u32[]{:S(2)}) copy-start(f32[128]{0:T(128)} %param.15) | copy-start | bytes 1540
  185.5 125.1 %copy-start.5 = (f32[128]{0:T(128)S(1)}, f32[128]{0:T(128)}, u32[]{:S(2)}) copy-start(f32[128]{0:T(128)} %param.16) | copy-start | bytes 1540
  185.5 125.5 %copy-start.2 = (bf16[128,128]{1,0:T(8,128)(2,1)S(1)}, bf16[128,128]{1,0:T(8,128)(2,1)}, u32[]{:S(2)}) copy-start(bf16[128,128]{1,0:T(8,128)(2,1)} %param.17) | copy-start | bytes 98308
  316.4 1.7 copy-start.1
  318.0 414.0 %reduce-scatter.5.cloned.1.call-start = ((), (), s32[]{:S(2)}) async-start(), calls=%async_computation.5 | async-start | bytes 4866048 | tf_op jit(solution)/shard_map/reduce_scatter | solution.py:127
Sparse Core Ops, SparseCore 0:
  184.2 122.0 all-gather.1
  318.1 160.6 reduce-scatter.6
  482.2 249.6 reduce-scatter.4
where the time goes:
time: 741 us; the launch traced here: 740 us
  waiting for transfers between devices  556 us (75%)
  blocking collectives  123 us (17%)
  starting transfers between devices  19.4 us (3%)
  matrix products  14 us (2%)
  between operations  14 us (2%)
  other arithmetic  7.63 us (1%)
    reduce_scatter x1, waiting for transfers between devices, on_device(): lax.psum_scatter(partial_w.astype(jnp.bfloat16), 'dp', scatter_dimension=...  252 us
    unnamed x4, waiting for transfers between devices  156 us
    psum x1, blocking collectives, on_device(): lax.psum((jnp.sum(values, axis=1), jnp.sum(values * values, axis=1)), 'mp')  123 us
    all_gather x1, waiting for transfers between devices, on_device(): gathered = lax.all_gather(normed, 'mp', axis=1, tiled=True)  121 us
    all_to_all x1, waiting for transfers between devices, on_device(): lax.all_to_all(outgoing.reshape(owners, CAP, shard_width), 'dp', split_ax...  16 us
    all_to_all x1, starting transfers between devices, on_device(): lax.all_to_all(slot_out.reshape(owners, CAP), 'dp', split_axis=0, concat_...  15.4 us
  transfers between devices with their start and end apart: 5, of which 5 were waited for; matrix products, arithmetic and copies ran while one was open for 1% of the time, Pallas kernels for 0%

commit v1 on v0

v1 whole, which is shorter than its diff:
```python
import functools
import math

import jax
import jax.numpy as jnp
from jax import lax
from jax.experimental import pallas as pl
from jax.experimental.pallas import tpu as pltpu
from jax.sharding import PartitionSpec as P

MESH = pl.DeviceIdType.MESH
F32 = jnp.float32
BF16 = jnp.bfloat16
HEAD = 128
ROWS = 128
ZL, X = 8, 4
ZH, Y, C = 4, 4, 2
SLOT = 16
HIGHEST = lax.Precision.HIGHEST


def dot(a, b, ca, cb, precision=None):
    return lax.dot_general(
        a, b, (((ca,), (cb,)), ((), ())), precision=precision, preferred_element_type=F32
    )


def rcopy(src, dst, ssem, rsem, dev):
    return pltpu.make_async_remote_copy(
        src_ref=src, dst_ref=dst, send_sem=ssem, recv_sem=rsem, device_id=dev, device_id_type=MESH
    )


class Ring:
    def __init__(self, n, p, dev):
        self.n, self.p = n, p
        self.right = lax.rem(p + 1, n)
        self.left = lax.rem(p + n - 1, n)
        self.opp = lax.rem(p + 2, n)
        self.dev_right, self.dev_left = dev(self.right), dev(self.left)

    def others(self):
        return {1: [], 2: [self.left], 4: [self.opp, self.left, self.right]}[self.n]

    def neighbours(self):
        return {1: [], 2: [self.dev_right], 4: [self.dev_left, self.dev_right]}[self.n]


class Gather:
    def __init__(self, ring, block, half, ss, rs, base):
        self.ring, self.block, self.half = ring, block, half
        self.ss, self.rs, self.base = ss, rs, base

    def _copy(self, ref, i, dev):
        return rcopy(ref, ref, self.ss.at[self.base + i], self.rs.at[self.base + i], dev)

    def _parts(self):
        g = self.ring
        if g.n == 1:
            return []
        if g.n == 2:
            return [(self.block(g.p), g.dev_right)]
        return [
            (self.block(g.p), g.dev_right),
            (self.block(g.p), g.dev_left),
            (self.half(g.left, 0), g.dev_right),
            (self.half(g.right, 1), g.dev_left),
        ]

    def send(self):
        for i, (ref, dev) in enumerate(self._parts()[:2]):
            self._copy(ref, i, dev).start()

    def relay(self):
        g = self.ring
        if g.n == 1:
            return
        self._copy(self.block(g.left), 0, g.dev_right).wait_recv()
        if g.n == 4:
            self._copy(self.half(g.left, 0), 2, g.dev_right).start()
            self._copy(self.block(g.right), 1, g.dev_left).wait_recv()
            self._copy(self.half(g.right, 1), 3, g.dev_left).start()

    def last(self):
        g = self.ring
        if g.n == 4:
            self._copy(self.half(g.opp, 0), 2, g.dev_right).wait_recv()
            self._copy(self.half(g.opp, 1), 3, g.dev_left).wait_recv()

    def drain(self):
        for i, (ref, dev) in enumerate(self._parts()):
            self._copy(ref, i, dev).wait_send()


class Scatter:
    def __init__(self, ring, block, half, bufs, ss, rs, base):
        self.ring, self.block, self.half, self.bufs = ring, block, half, bufs
        self.ss, self.rs, self.base = ss, rs, base

    def _copy(self, ref, i, dev):
        return rcopy(ref, self.bufs[i], self.ss.at[self.base + i], self.rs.at[self.base + i], dev)

    def _parts(self):
        g = self.ring
        if g.n == 1:
            return []
        if g.n == 2:
            return [(2, self.block(g.right), g.dev_right)]
        return [
            (0, self.half(g.opp, 0), g.dev_right),
            (1, self.half(g.opp, 1), g.dev_left),
            (2, self.block(g.right), g.dev_right),
            (3, self.block(g.left), g.dev_left),
        ]

    def first(self):
        for i, ref, dev in self._parts():
            if i < 2:
                self._copy(ref, i, dev).start()

    def second(self):
        g = self.ring
        if g.n == 4:
            self._copy(self.bufs[0], 0, g.dev_right).wait_recv()
            add_to(self.half(g.right, 0), self.bufs[0])
        if g.n > 1:
            self._copy(self.block(g.right), 2, g.dev_right).start()
        if g.n == 4:
            self._copy(self.bufs[1], 1, g.dev_left).wait_recv()
            add_to(self.half(g.left, 1), self.bufs[1])
            self._copy(self.block(g.left), 3, g.dev_left).start()

    def total(self):
        g = self.ring
        out = self.block(g.p)[...].astype(F32)
        if g.n > 1:
            self._copy(self.bufs[2], 2, g.dev_right).wait_recv()
            out = out + self.bufs[2][...].astype(F32)
        if g.n == 4:
            self._copy(self.bufs[3], 3, g.dev_left).wait_recv()
            out = out + self.bufs[3][...].astype(F32)
        return out

    def drain(self):
        for i, ref, dev in self._parts():
            self._copy(ref, i, dev).wait_send()


def add_to(ref, other):
    ref[...] = (ref[...].astype(F32) + other[...].astype(F32)).astype(ref.dtype)


def mean_of(v):
    return jnp.mean(v, axis=1, keepdims=True)


def norm_head(vector, gain_row):
    center = vector - mean_of(vector)
    inverse = lax.rsqrt(mean_of(center * center) + 1e-06)
    unit_rows = center * inverse
    return unit_rows * gain_row, unit_rows, inverse


def norm_head_back(cotangent, unit_rows, inverse, gain_row):
    scaled = cotangent * gain_row
    return inverse * (scaled - mean_of(scaled) - unit_rows * mean_of(scaled * unit_rows))


def head_pass(projected, gain_query, gain_key, allowed, cotangent):
    value_rows = projected[:, 2 * HEAD :]
    query_n, query_u, query_r = norm_head(projected[:, :HEAD].astype(F32), gain_query)
    key_n, key_u, key_r = norm_head(projected[:, HEAD : 2 * HEAD].astype(F32), gain_key)
    factor = 1.0 / math.sqrt(HEAD)
    scores = dot(query_n, key_n, 1, 1, HIGHEST) * factor
    scores = jnp.where(allowed, scores, -1e30)
    shifted = jnp.exp(scores - jnp.max(scores, axis=1, keepdims=True))
    softmax_rows = shifted / jnp.sum(shifted, axis=1, keepdims=True)
    probs_low = softmax_rows.astype(BF16)
    attended = dot(probs_low, value_rows, 1, 0).astype(BF16)
    grad_value = dot(probs_low, cotangent, 0, 0)
    grad_probs = dot(cotangent, value_rows, 1, 1)
    grad_scores = softmax_rows * (
        grad_probs - jnp.sum(grad_probs * softmax_rows, axis=1, keepdims=True)
    )
    grad_qn = dot(grad_scores, key_n, 1, 0, HIGHEST) * factor
    grad_kn = dot(grad_scores, query_n, 0, 0, HIGHEST) * factor
    grad_query = norm_head_back(grad_qn, query_u, query_r, gain_query)
    grad_key = norm_head_back(grad_kn, key_u, key_r, gain_key)
    return attended, jnp.concatenate([grad_query, grad_key, grad_value], axis=1).astype(BF16)


def kernel(
    patches_ref, owner_ref, slot_ref, seg_ref, gain_ref, w_hbm, qg_ref, kg_ref, cot_ref,
    attn_ref, ng_ref, wg_ref,
    w_ref, gb_ref, pt_ref, out_buf, arr, gath, nt, br, ga, ts, cr, ya, yb, yl, yr, qb, za, zb, zl_, zr_,
    w_sem, a2a_s, a2a_r, hg_s, hg_r, yg_s, yg_r, cg_s, cg_r, nt_s, nt_r, ny_s, ny_r, nc_s, nc_r,
    zg_s, zg_r, xg_s, xg_r, ca_s, ca_r, yr_s, yr_r, hr_s, hr_r,
):
    n_dp, n_mp = ZL * X, ZH * Y * C
    feats = patches_ref.shape[0]
    width = n_mp * feats
    fy = feats // Y
    per_class = n_dp // C
    d, m = lax.axis_index("dp"), lax.axis_index("mp")
    z, x = lax.div(d, X), lax.rem(d, X)
    h, y, c = lax.div(m, Y * C), lax.rem(lax.div(m, C), Y), lax.rem(m, C)
    ring_h = Ring(ZH, h, lambda q: (d, (q * Y + y) * C + c))
    ring_y = Ring(Y, y, lambda q: (d, (h * Y + q) * C + c))
    ring_x = Ring(X, x, lambda q: (z * X + q, m))
    twin = (d, (h * Y + y) * C + (1 - c))
    other = 1 - c

    load_w = pltpu.make_async_copy(w_hbm, w_ref, w_sem)
    load_w.start()

    barrier = pltpu.get_barrier_semaphore()

    def hail(k, _):
        to = lax.rem(d + k, n_dp)
        pl.semaphore_signal(barrier, inc=1, device_id=(to, m), device_id_type=MESH)
        return 0

    lax.fori_loop(1, n_dp, hail, 0)
    near = ring_h.neighbours() + ring_y.neighbours() + ([twin] if C == 2 else [])
    for dev in near:
        pl.semaphore_signal(barrier, inc=1, device_id=dev, device_id_type=MESH)

    owners = jnp.broadcast_to(owner_ref[...].astype(F32), (ROWS, ROWS))
    rows_i = lax.broadcasted_iota(jnp.int32, (ROWS, ROWS), 0)
    cols_i = lax.broadcasted_iota(jnp.int32, (ROWS, ROWS), 1)
    same = jnp.where((owners == owners.T) & (rows_i < cols_i), 1.0, 0.0)
    rank = jnp.sum(same, axis=0, keepdims=True)
    target = owner_ref[...].astype(F32) * SLOT + rank
    slots_i = lax.broadcasted_iota(jnp.int32, (n_dp * SLOT, ROWS), 0).astype(F32)
    pick = jnp.where(slots_i == target, 1.0, 0.0).astype(BF16)
    pt_ref[:feats] = patches_ref[...]
    pt_ref[feats:] = jnp.broadcast_to(
        slot_ref[...].astype(F32) + 1.0, (pt_ref.shape[0] - feats, ROWS)
    ).astype(BF16)
    outgoing = dot(pick, pt_ref[...], 1, 1).astype(BF16)
    out_buf[...] = outgoing.reshape(out_buf.shape)

    pl.semaphore_wait(barrier, n_dp - 1 + len(near))

    def a2a_send(k, _):
        to = lax.rem(d + k, n_dp)
        rcopy(out_buf.at[to], arr.at[d], a2a_s.at[to], a2a_r.at[d], (to, m)).start()
        return 0

    lax.fori_loop(1, n_dp, a2a_send, 0)
    arr[d] = out_buf[d]

    def spread_gain(j, _):
        tile = jnp.broadcast_to(gain_ref[pl.ds(j, 1), :], (128, 128))
        gb_ref[pl.ds(pl.multiple_of(j * 128, 128), 128), :] = tile.T
        return 0

    lax.fori_loop(0, width // 128, spread_gain, 0)

    def a2a_wait(k, _):
        frm = lax.rem(d + n_dp - k, n_dp)
        rcopy(out_buf.at[frm], arr.at[frm], a2a_s.at[frm], a2a_r.at[frm], (frm, m)).wait_recv()
        return 0

    lax.fori_loop(1, n_dp, a2a_wait, 0)
    arrived = arr[...].reshape(n_dp * SLOT, arr.shape[2])
    lanes = lax.broadcasted_iota(jnp.int32, (n_dp * SLOT, ROWS), 1).astype(F32) + 1.0
    place = jnp.where(
        lanes == arrived[:, feats : feats + 1].astype(F32), 1.0, 0.0
    ).astype(BF16)
    gath[m] = dot(arrived[:, :feats], place, 0, 0).astype(BF16)

    g_h = Gather(
        ring_h,
        lambda q: gath.at[(q * Y + y) * C + c],
        lambda q, i: gath.at[(q * Y + y) * C + c, pl.ds(i * (feats // 2), feats // 2)],
        hg_s, hg_r, 0,
    )

    def gather_y(idx, hh):
        return Gather(
            ring_y,
            lambda q: gath.at[(hh * Y + q) * C + c],
            lambda q, i: gath.at[(hh * Y + q) * C + c, pl.ds(i * (feats // 2), feats // 2)],
            yg_s, yg_r, idx * 4,
        )

    def twin_copy(idx, hh, q, core):
        ref = gath.at[(hh * Y + q) * C + core]
        i = idx * Y + q
        return rcopy(ref, ref, cg_s.at[i], cg_r.at[i], twin)

    def to_twin(idx, hh, qs):
        if C == 2:
            for q in qs:
                twin_copy(idx, hh, q, c).start()

    come = [h] + {1: [], 2: [ring_h.left], 4: [ring_h.left, ring_h.right, ring_h.opp]}[ZH]
    g_y = [gather_y(i, hh) for i, hh in enumerate(come)]
    near_y = {1: [], 2: [ring_y.left], 4: [ring_y.left, ring_y.right]}[Y]
    far_y = [ring_y.opp] if Y == 4 else []

    def own_y(i):
        g_y[i].send()
        to_twin(i, come[i], [y])

    def next_y(i):
        g_y[i].relay()
        to_twin(i, come[i], near_y)

    def last_y(i):
        g_y[i].last()
        to_twin(i, come[i], far_y)

    g_h.send()
    own_y(0)
    next_y(0)
    g_h.relay()
    for i in range(1, min(len(come), 3)):
        own_y(i)
    last_y(0)
    g_h.last()
    if ZH == 4:
        own_y(3)
    for i in range(1, len(come)):
        next_y(i)
    for i in range(1, len(come)):
        last_y(i)
    if C == 2:
        for i, hh in enumerate(come):
            for q in range(Y):
                twin_copy(i, hh, q, other).wait_recv()

    def sums(j, carry):
        s1, s2 = carry
        v = gath[j].astype(F32).reshape(feats // 8, 8, ROWS)
        return s1 + jnp.sum(v, axis=0), s2 + jnp.sum(v * v, axis=0)

    zero = jnp.zeros((8, ROWS), F32)
    s1, s2 = lax.fori_loop(0, n_mp, sums, (zero, zero))
    row_mean = jnp.sum(s1, axis=0, keepdims=True) / width
    row_var = jnp.sum(s2, axis=0, keepdims=True) / width - row_mean * row_mean
    inverse = lax.rsqrt(row_var + 1e-06)

    load_w.wait()
    step = 4

    def project(j, acc):
        v = gath[pl.ds(j * step, step)].astype(F32).reshape(step * feats, ROWS)
        rows = pl.ds(pl.multiple_of(j * (step * feats), step * feats), step * feats)
        low = ((v - row_mean) * inverse * gb_ref[rows, :]).astype(BF16)
        nt[pl.ds(j * step, step)] = low.reshape(step, feats, ROWS)
        return acc + dot(low, w_ref[rows, :], 0, 0)

    projected = lax.fori_loop(
        0, n_mp // step, project, jnp.zeros((ROWS, 3 * HEAD), F32)
    ).astype(BF16)

    mine = lax.rem(c + C * n_dp - d, C)

    def nt_copy(i, to):
        return rcopy(
            nt.at[to, pl.ds(pl.multiple_of(y * fy, fy), fy)],
            br.at[y, c, lax.div(d, C)],
            nt_s.at[i], nt_r.at[lax.div(d, C)], (to, m),
        )

    def nt_send(k, _):
        i = lax.rem(lax.div(d, C) + k, per_class)
        to = i * C + mine

        @pl.when(to != d)
        def _():
            nt_copy(i, to).start()

        return 0

    lax.fori_loop(0, per_class, nt_send, 0)

    @pl.when(mine == lax.rem(d, C))
    def _():
        br[y, c, lax.div(d, C)] = nt[d, pl.ds(pl.multiple_of(y * fy, fy), fy)]

    seg = jnp.broadcast_to(seg_ref[...].astype(F32), (ROWS, ROWS))
    attended, grads = head_pass(
        projected, qg_ref[...], kg_ref[...], seg == seg.T, cot_ref[...]
    )
    ga[d] = grads

    def z_copy(level, up):
        dev = (d + X, m) if up else (d - X, m)
        ref = ga.at[level * X + x]
        i = level + (ZL if up else 0)
        return rcopy(ref, ref, zg_s.at[i], zg_r.at[level], dev)

    def z_wait(level):
        ref = ga.at[level * X + x]
        dev = (lax.rem(d + X, n_dp), m)
        rcopy(ref, ref, zg_s.at[level], zg_r.at[level], dev).wait_recv()

    def gather_x(level):
        return Gather(
            ring_x,
            lambda q: ga.at[level * X + q],
            lambda q, i: ga.at[level * X + q, pl.ds(i * (ROWS // 2), ROWS // 2)],
            xg_s, xg_r, level * 4,
        )

    def levels(k, fn):
        @pl.when(z >= k)
        def _():
            fn(z - k, True)

        @pl.when(z + k < ZL)
        def _():
            fn(z + k, False)

    def z_step(level, below):
        z_wait(level)
        if below:

            @pl.when(z < ZL - 1)
            def _():
                z_copy(level, True).start()
        else:

            @pl.when(z > 0)
            def _():
                z_copy(level, False).start()

        gather_x(level).send()

    @pl.when(z < ZL - 1)
    def _():
        z_copy(z, True).start()

    @pl.when(z > 0)
    def _():
        z_copy(z, False).start()

    gather_x(z).send()
    attn_ref[...] = attended

    order = ring_h.others() + [h]

    def term(idx):
        hh = order[idx]
        rows = Y * C * feats
        block = dot(w_ref[pl.ds(pl.multiple_of(hh * rows, rows), rows), :], grads, 1, 1)
        block = block.astype(BF16)
        for q in range(Y):
            for core in range(C):
                at = (q * C + core) * feats
                ts[hh, core, q] = block[at : at + feats]
        if C == 2:
            core_copy(idx).start()

    def core_copy(idx):
        return rcopy(ts.at[order[idx], other], cr.at[idx], ca_s.at[idx], ca_r.at[idx], twin)

    def scatter_y(idx):
        hh = order[idx]
        return Scatter(
            ring_y,
            lambda q: ts.at[hh, c, q],
            lambda q, i: ts.at[hh, c, q, pl.ds(i * (feats // 2), feats // 2)],
            [ya.at[idx], yb.at[idx], yl.at[idx], yr.at[idx]],
            yr_s, yr_r, idx * 4,
        )

    s_y = [scatter_y(i) for i in range(len(order))]
    s_h = Scatter(
        ring_h,
        lambda q: qb.at[q],
        lambda q, i: qb.at[q, pl.ds(i * (feats // 2), feats // 2)],
        [za, zb, zl_, zr_],
        hr_s, hr_r, 0,
    )

    def rs_a(idx):
        if C == 2:
            core_copy(idx).wait_recv()
            add_to(ts.at[order[idx], c], cr.at[idx])
        s_y[idx].first()

    def rs_b(idx):
        s_y[idx].second()

    def rs_c(idx):
        qb[order[idx]] = s_y[idx].total().astype(BF16)

    for i in range(len(order)):
        term(i)

    g_n = Gather(
        ring_y,
        lambda q: br.at[q, c],
        lambda q, i: br.at[q, c, pl.ds(i * (per_class // 2), per_class // 2)],
        ny_s, ny_r, 0,
    )

    def n_copy(q, core):
        return rcopy(br.at[q, core], br.at[q, core], nc_s.at[q], nc_r.at[q], twin)

    def n_wait(k, _):
        i = lax.rem(lax.div(d, C) + per_class - k, per_class)

        @pl.when(i * C + mine != d)
        def _():
            rcopy(
                br.at[y, c, i], br.at[y, c, i], nt_s.at[i], nt_r.at[i], (lax.rem(d + 1, n_dp), m)
            ).wait_recv()

        return 0

    def n_to_twin(qs):
        if C == 2:
            for q in qs:
                n_copy(q, c).start()

    def n_first():
        lax.fori_loop(0, per_class, n_wait, 0)
        g_n.send()
        n_to_twin([y])

    def n_second():
        g_n.relay()
        n_to_twin(near_y)

    def n_third():
        g_n.last()
        n_to_twin(far_y)

    def n_last():
        if C == 2:
            for q in range(Y):
                n_copy(q, other).wait_recv()

    every = range(len(order))
    jobs = [
        [functools.partial(rs_a, i) for i in every] + [n_first],
        [functools.partial(rs_b, i) for i in every],
        [functools.partial(rs_c, i) for i in every] + [s_h.first, n_second],
        [s_h.second, n_third],
        [n_last],
    ]
    jobs = jobs + [[]] * (ZL - 1 - len(jobs))
    span = max(ZL - 1, 1)
    for k in range(1, ZL):
        levels(k, z_step)
        share = jobs[(k - 1) * len(jobs) // span : k * len(jobs) // span]
        for group in share:
            for job in group:
                job()
        if k == 1:
            gather_x(z).relay()
        else:
            levels(k - 1, lambda level, _: gather_x(level).relay())
    if ZL == 1:
        for group in jobs:
            for job in group:
                job()
        gather_x(z).relay()
    else:
        levels(ZL - 1, lambda level, _: gather_x(level).relay())

    wg_ref[...] = jnp.zeros_like(wg_ref)

    def weight_term(level):
        gather_x(level).last()
        left = []
        for q in range(X):
            src = level * X + q
            kind = lax.rem(d + src, C)
            left.append(br[:, kind, lax.div(src, C)].reshape(feats, ROWS))
        right = ga[pl.ds(level * X, X)].reshape(X * ROWS, 3 * HEAD)
        wg_ref[...] += dot(jnp.concatenate(left, axis=1), right, 1, 0)

    weight_term(z)

    def weight_step(k, _):
        levels(k, lambda level, _: weight_term(level))
        return 0

    lax.fori_loop(1, ZL, weight_step, 0)
    ng_ref[...] = s_h.total()

    def a2a_drain(k, _):
        to = lax.rem(d + k, n_dp)
        rcopy(out_buf.at[to], arr.at[d], a2a_s.at[to], a2a_r.at[d], (to, m)).wait_send()
        return 0

    lax.fori_loop(1, n_dp, a2a_drain, 0)
    g_h.drain()
    for g in g_y:
        g.drain()
    if C == 2:
        for i, hh in enumerate(come):
            for q in range(Y):
                twin_copy(i, hh, q, c).wait_send()

    def nt_drain(i, _):
        @pl.when(i * C + mine != d)
        def _():
            nt_copy(i, i * C + mine).wait_send()

        return 0

    lax.fori_loop(0, per_class, nt_drain, 0)
    g_n.drain()
    if C == 2:
        for q in range(Y):
            n_copy(q, c).wait_send()
        for i in every:
            core_copy(i).wait_send()
    for i in every:
        s_y[i].drain()
    s_h.drain()

    @pl.when(z < ZL - 1)
    def _():
        z_copy(z, True).wait_send()

    @pl.when(z > 0)
    def _():
        z_copy(z, False).wait_send()

    gather_x(z).drain()

    def far_drain(level, below):
        @pl.when((z < ZL - 1) if below else (z > 0))
        def _():
            z_copy(level, below).wait_send()

        gather_x(level).drain()

    def z_drain(k, _):
        levels(k, far_drain)
        return 0

    lax.fori_loop(1, ZL, z_drain, 0)


def on_device(
    patches, route_owner, route_slot, segment_ids, ln_gain, qkv_weight, q_gain, k_gain, d_attn
):
    n_dp, n_mp = ZL * X, ZH * Y * C
    feats = patches.shape[1]
    width = qkv_weight.shape[0]
    ext = -(-(feats + 1) // 128) * 128
    vmem = pl.BlockSpec(memory_space=pltpu.VMEM)
    dma = lambda n: pltpu.SemaphoreType.DMA((max(n, 1),))
    half = feats // 2
    pairs = []
    for n in (n_dp, 4, 4 * ZH, ZH * Y, n_dp // C, 4, Y):
        pairs += [dma(n), dma(n)]
    pairs += [dma(2 * ZL), dma(ZL), dma(4 * ZL), dma(4 * ZL)]
    for n in (ZH, 4 * ZH, 4):
        pairs += [dma(n), dma(n)]
    return pl.pallas_call(
        kernel,
        out_shape=(
            jax.ShapeDtypeStruct((ROWS, HEAD), BF16),
            jax.ShapeDtypeStruct((feats, ROWS), F32),
            jax.ShapeDtypeStruct((width // n_dp, 3 * HEAD), F32),
        ),
        in_specs=[vmem] * 5 + [pl.BlockSpec(memory_space=pl.ANY)] + [vmem] * 3,
        out_specs=(vmem, vmem, vmem),
        scratch_shapes=[
            pltpu.VMEM((width, 3 * HEAD), BF16),
            pltpu.VMEM((width, 128), F32),
            pltpu.VMEM((ext, ROWS), BF16),
            pltpu.VMEM((n_dp, SLOT, ext), BF16),
            pltpu.VMEM((n_dp, SLOT, ext), BF16),
            pltpu.VMEM((n_mp, feats, ROWS), BF16),
            pltpu.VMEM((n_mp, feats, ROWS), BF16),
            pltpu.VMEM((Y, C, n_dp // C, feats // Y, ROWS), BF16),
            pltpu.VMEM((n_dp, ROWS, 3 * HEAD), BF16),
            pltpu.VMEM((ZH, C, Y, feats, ROWS), BF16),
            pltpu.VMEM((ZH, Y, feats, ROWS), BF16),
            pltpu.VMEM((ZH, half, ROWS), BF16),
            pltpu.VMEM((ZH, half, ROWS), BF16),
            pltpu.VMEM((ZH, feats, ROWS), BF16),
            pltpu.VMEM((ZH, feats, ROWS), BF16),
            pltpu.VMEM((ZH, feats, ROWS), BF16),
            pltpu.VMEM((half, ROWS), BF16),
            pltpu.VMEM((half, ROWS), BF16),
            pltpu.VMEM((feats, ROWS), BF16),
            pltpu.VMEM((feats, ROWS), BF16),
            pltpu.SemaphoreType.DMA,
            *pairs,
        ],
        compiler_params=pltpu.CompilerParams(
            collective_id=0, has_side_effects=True, vmem_limit_bytes=48 * 1024 * 1024
        ),
    )(
        patches.T,
        route_owner.reshape(1, ROWS),
        route_slot.reshape(1, ROWS),
        segment_ids,
        ln_gain.reshape(width // 128, 128),
        qkv_weight,
        q_gain.reshape(1, HEAD),
        k_gain.reshape(1, HEAD),
        d_attn,
    )


def solution(mesh):
    in_specs = (
        P("dp", "mp"),
        P("dp"),
        P("dp"),
        P("dp", None),
        P(),
        P(None, "mp"),
        P("mp"),
        P("mp"),
        P("dp", "mp"),
    )
    out_specs = (P("dp", "mp"), P("mp", "dp"), P("dp", "mp"))
    return jax.shard_map(
        on_device, mesh=mesh, in_specs=in_specs, out_specs=out_specs, check_vma=False
    )
```

time: 741 us -> 140 us (0.19)
  waiting for transfers between devices: 556 us -> 0 us
  Pallas kernels: 0 us -> 127 us
  blocking collectives: 123 us -> 0 us
  starting transfers between devices: 19.4 us -> 0 us
  matrix products: 14 us -> 0 us
  between operations: 14 us -> 0.66 us
  other arithmetic: 7.63 us -> 0 us
    reduce_scatter x1 -> x0, waiting for transfers between devices: 252 us -> none  [on_device(): lax.psum_scatter(partial_w.astype(jnp.bfloat16), 'dp', scatter_dimension=...]
    unnamed x4 -> x0, waiting for transfers between devices: 156 us -> none
    pallas_call x0 -> x1, Pallas kernels: none -> 127 us  [on_device(): pl.pallas_call(kernel, out_shape=(jax.ShapeDtypeStruct((ROWS, HEAD), BF16...]
    psum x1 -> x0, blocking collectives: 123 us -> none  [on_device(): lax.psum((jnp.sum(values, axis=1), jnp.sum(values * values, axis=1)), 'mp')]
    all_gather x1 -> x0, waiting for transfers between devices: 121 us -> none  [on_device(): gathered = lax.all_gather(normed, 'mp', axis=1, tiled=True)]
    all_to_all x2 -> x0, waiting for transfers between devices: 27.3 us -> none  [the longest x1 16 us: on_device(): lax.all_to_all(outgoing.reshape(owners, CAP, shard_width), 'dp', split_ax...]
    all_to_all x2 -> x0, starting transfers between devices: 19.2 us -> none  [the longest x1 15.4 us: on_device(): lax.all_to_all(slot_out.reshape(owners, CAP), 'dp', split_axis=0, concat_...]
    dot_general x11 -> x0, matrix products: 14 us -> none  [the longest x1 3.92 us: on_device(): lax.dot_general(qkv_weight, grads, (((1,), (1,)), ((), ())), preferred_el...]
  transfers between devices with their start and end apart: 5 -> 0, of which waited for: 5 -> 0; matrix products, arithmetic and copies ran while one was open for 1% -> 0% of each run, Pallas kernels for 0% -> 0%
where the time goes in v1:
time: 140 us; the launch traced here: 138 us
  Pallas kernels  127 us (91%)
  local copies, waits for them, and re-layouts  9.87 us (7%)
    pallas_call x1, Pallas kernels, on_device(): pl.pallas_call(kernel, out_shape=(jax.ShapeDtypeStruct((ROWS, HEAD), BF16...  127 us
    unnamed x21, local copies, waits for them, and re-layouts  9.87 us

profile of v1, /device:TPU:24, one launch (start us, length us, event | category | flops | bytes accessed | tf_op | source)
XLA Modules:
  0.0 137.6 jit_solution(15644354408835281240)
XLA Ops:
  0.6 0.0 copy-start
  0.6 2.3 %copy-done = bf16[6144,384]{1,0:T(8,128)(2,1)S(1)} copy-done((bf16[6144,384]{1,0:T(8,128)(2,1)S(1)}, bf16[6144,384]{1,0:T(8,128)(2,1)}, u32[]{:S(2)}) %copy-start) | copy-done | bytes 4718616
  3.0 0.0 copy-start.1
  3.0 0.8 copy-done.1
  3.8 0.0 copy-start.2
  3.8 0.8 copy-done.2
  4.5 0.0 copy-start.3
  4.5 0.7 copy-done.3
  5.3 0.0 copy-start.4
  5.3 0.7 copy-done.4
  5.9 0.0 copy-start.5
  5.9 0.7 copy-done.5
  6.6 0.0 copy-start.6
  6.6 0.7 copy-done.6
  7.2 0.0 copy-start.7
  7.2 0.7 copy-done.7
  7.9 0.0 copy-start.8
  7.9 0.7 copy-done.8
  8.5 127.1 %shard_map.112 = (bf16[128,128]{1,0:T(8,128)(2,1)S(1)}, f32[192,128]{1,0:T(8,128)S(1)}, f32[192,384]{1,0:T(8,128)S(1)}) custom-call(bf16[192,128]{1,0:T(8,128)(2,1)S(1)} %bitcast.6, s32[1,128]{1,0:T(1,128)S(1)} %bitcast.8, s32[1,128]{1,0:T(1,128)S(1)} %bitcast.9, s32[1,128]{1,0:T(1,128)S(1)} %copy-done.6, f32[48,128]{1,0:T(8,128)S(1)} %bitcast.7, ...), custom_call_target="tpu_custom_call" | custom-call | tf_op jit(solution)/shard_map/pallas_call | solution.py:660
  135.6 0.6 copy.15
  136.2 0.6 copy.16
  136.9 0.7 copy.17
Async XLA Ops:
  0.6 2.3 %copy-start = (bf16[6144,384]{1,0:T(8,128)(2,1)S(1)}, bf16[6144,384]{1,0:T(8,128)(2,1)}, u32[]{:S(2)}) copy-start(bf16[6144,384]{1,0:T(8,128)(2,1)} %w_hbm.1) | copy-start | bytes 14155780
  3.0 0.8 copy-start.1
  3.8 0.8 copy-start.2
  4.5 0.7 copy-start.3
  5.3 0.7 copy-start.4
  5.9 0.7 copy-start.5
  6.6 0.7 copy-start.6
  7.2 0.7 copy-start.7
  7.9 0.7 copy-start.8

commit v2 on v1

--- a/solution.py
+++ b/solution.py
@@ -15,6 +15,7 @@
 ROWS = 128
 ZL, X = 8, 4
 ZH, Y, C = 4, 4, 2
+EXPRESS = 4
 SLOT = 16
 HIGHEST = lax.Precision.HIGHEST
 
@@ -47,103 +48,124 @@
 
 
 class Gather:
+    SENDS = 6
+
     def __init__(self, ring, block, half, ss, rs, base):
         self.ring, self.block, self.half = ring, block, half
-        self.ss, self.rs, self.base = ss, rs, base
+        self.ss, self.rs, self.base = ss, rs, base * self.SENDS
 
     def _copy(self, ref, i, dev):
         return rcopy(ref, ref, self.ss.at[self.base + i], self.rs.at[self.base + i], dev)
 
-    def _parts(self):
+    def _sent(self):
         g = self.ring
         if g.n == 1:
             return []
         if g.n == 2:
-            return [(self.block(g.p), g.dev_right)]
+            return [lambda: self._copy(self.block(g.p), 0, g.dev_right)]
         return [
-            (self.block(g.p), g.dev_right),
-            (self.block(g.p), g.dev_left),
-            (self.half(g.left, 0), g.dev_right),
-            (self.half(g.right, 1), g.dev_left),
+            lambda: self._copy(self.half(g.p, 0), 0, g.dev_right),
+            lambda: self._copy(self.half(g.p, 1), 1, g.dev_left),
+            lambda: self._copy(self.half(g.p, 1), 2, g.dev_right),
+            lambda: self._copy(self.half(g.p, 0), 3, g.dev_left),
+            lambda: self._copy(self.half(g.left, 0), 4, g.dev_right),
+            lambda: self._copy(self.half(g.right, 1), 5, g.dev_left),
         ]
 
     def send(self):
-        for i, (ref, dev) in enumerate(self._parts()[:2]):
-            self._copy(ref, i, dev).start()
+        for copy in self._sent()[:4]:
+            copy().start()
 
     def relay(self):
         g = self.ring
-        if g.n == 1:
-            return
-        self._copy(self.block(g.left), 0, g.dev_right).wait_recv()
         if g.n == 4:
-            self._copy(self.half(g.left, 0), 2, g.dev_right).start()
-            self._copy(self.block(g.right), 1, g.dev_left).wait_recv()
-            self._copy(self.half(g.right, 1), 3, g.dev_left).start()
+            sent = self._sent()
+            self._copy(self.half(g.left, 0), 0, g.dev_right).wait_recv()
+            sent[4]().start()
+            self._copy(self.half(g.right, 1), 1, g.dev_left).wait_recv()
+            sent[5]().start()
+
+    def rest(self):
+        g = self.ring
+        if g.n == 2:
+            self._copy(self.block(g.left), 0, g.dev_right).wait_recv()
+        if g.n == 4:
+            self._copy(self.half(g.left, 1), 2, g.dev_right).wait_recv()
+            self._copy(self.half(g.right, 0), 3, g.dev_left).wait_recv()
 
     def last(self):
         g = self.ring
         if g.n == 4:
-            self._copy(self.half(g.opp, 0), 2, g.dev_right).wait_recv()
-            self._copy(self.half(g.opp, 1), 3, g.dev_left).wait_recv()
+            self._copy(self.half(g.opp, 0), 4, g.dev_right).wait_recv()
+            self._copy(self.half(g.opp, 1), 5, g.dev_left).wait_recv()
 
     def drain(self):
-        for i, (ref, dev) in enumerate(self._parts()):
-            self._copy(ref, i, dev).wait_send()
+        for copy in self._sent():
+            copy().wait_send()
 
 
 class Scatter:
+    SENDS = 6
+
     def __init__(self, ring, block, half, bufs, ss, rs, base):
         self.ring, self.block, self.half, self.bufs = ring, block, half, bufs
-        self.ss, self.rs, self.base = ss, rs, base
-
-    def _copy(self, ref, i, dev):
-        return rcopy(ref, self.bufs[i], self.ss.at[self.base + i], self.rs.at[self.base + i], dev)
-
-    def _parts(self):
-        g = self.ring
+        self.ss, self.rs, self.base = ss, rs, base * self.SENDS
+
+    def _copy(self, ref, dst, i, dev):
+        return rcopy(ref, dst, self.ss.at[self.base + i], self.rs.at[self.base + i], dev)
+
+    def _sent(self):
+        g, b = self.ring, self.bufs
         if g.n == 1:
             return []
         if g.n == 2:
-            return [(2, self.block(g.right), g.dev_right)]
+            return [lambda: self._copy(self.block(g.right), b[2], 0, g.dev_right)]
         return [
-            (0, self.half(g.opp, 0), g.dev_right),
-            (1, self.half(g.opp, 1), g.dev_left),
-            (2, self.block(g.right), g.dev_right),
-            (3, self.block(g.left), g.dev_left),
+            lambda: self._copy(self.half(g.opp, 0), b[0], 0, g.dev_right),
+            lambda: self._copy(self.half(g.opp, 1), b[1], 1, g.dev_left),
+            lambda: self._copy(self.half(g.right, 1), self._part(b[2], 1), 2, g.dev_right),
+            lambda: self._copy(self.half(g.left, 0), self._part(b[3], 0), 3, g.dev_left),
+            lambda: self._copy(self.half(g.right, 0), self._part(b[2], 0), 4, g.dev_right),
+            lambda: self._copy(self.half(g.left, 1), self._part(b[3], 1), 5, g.dev_left),
         ]
 
+    @staticmethod
+    def _part(ref, i):
+        rows = ref.shape[0] // 2
+        return ref.at[pl.ds(i * rows, rows)]
+
     def first(self):
-        for i, ref, dev in self._parts():
-            if i < 2:
-                self._copy(ref, i, dev).start()
+        for copy in self._sent()[:4]:
+            copy().start()
 
     def second(self):
         g = self.ring
         if g.n == 4:
-            self._copy(self.bufs[0], 0, g.dev_right).wait_recv()
+            sent = self._sent()
+            sent[0]().wait_recv()
             add_to(self.half(g.right, 0), self.bufs[0])
+            sent[4]().start()
+            sent[1]().wait_recv()
+            add_to(self.half(g.left, 1), self.bufs[1])
+            sent[5]().start()
+
+    def total(self):
+        g, sent = self.ring, self._sent()
+        out = self.block(g.p)[...].astype(F32)
+        if g.n == 2:
+            sent[0]().wait_recv()
+        if g.n == 4:
+            for i in (2, 3, 4, 5):
+                sent[i]().wait_recv()
         if g.n > 1:
-            self._copy(self.block(g.right), 2, g.dev_right).start()
-        if g.n == 4:
-            self._copy(self.bufs[1], 1, g.dev_left).wait_recv()
-            add_to(self.half(g.left, 1), self.bufs[1])
-            self._copy(self.block(g.left), 3, g.dev_left).start()
-
-    def total(self):
-        g = self.ring
-        out = self.block(g.p)[...].astype(F32)
-        if g.n > 1:
-            self._copy(self.bufs[2], 2, g.dev_right).wait_recv()
             out = out + self.bufs[2][...].astype(F32)
         if g.n == 4:
-            self._copy(self.bufs[3], 3, g.dev_left).wait_recv()
             out = out + self.bufs[3][...].astype(F32)
         return out
 
     def drain(self):
-        for i, ref, dev in self._parts():
-            self._copy(ref, i, dev).wait_send()
+        for copy in self._sent():
+            copy().wait_send()
 
 
 def add_to(ref, other):
@@ -190,17 +212,19 @@
 
 
 def kernel(
-    patches_ref, owner_ref, slot_ref, seg_ref, gain_ref, w_hbm, qg_ref, kg_ref, cot_ref,
+    patches_hbm, owner_hbm, slot_hbm, seg_hbm, gain_hbm, w_hbm, qg_hbm, kg_hbm, cot_hbm,
     attn_ref, ng_ref, wg_ref,
-    w_ref, gb_ref, pt_ref, out_buf, arr, gath, nt, br, ga, ts, cr, ya, yb, yl, yr, qb, za, zb, zl_, zr_,
-    w_sem, a2a_s, a2a_r, hg_s, hg_r, yg_s, yg_r, cg_s, cg_r, nt_s, nt_r, ny_s, ny_r, nc_s, nc_r,
-    zg_s, zg_r, xg_s, xg_r, ca_s, ca_r, yr_s, yr_r, hr_s, hr_r,
+    patches_ref, owner_ref, slot_ref, seg_ref, gain_ref, w_ref, qg_ref, kg_ref, cot_ref,
+    gb_ref, pt_ref, out_buf, arr, gath, nt, br, ga, ts, cr, ya, yb, yl, yr, qb, za, zb, zl_, zr_,
+    wa, wb, xa, xb, xl, xr,
+    in_sem, a2a_s, a2a_r, hg_s, hg_r, yg_s, yg_r, cg_s, cg_r, nt_s, nt_r, ny_s, ny_r, nc_s, nc_r,
+    zg_s, zg_r, xs_s, xs_r, ca_s, ca_r, yr_s, yr_r, hr_s, hr_r,
 ):
     n_dp, n_mp = ZL * X, ZH * Y * C
-    feats = patches_ref.shape[0]
+    feats = patches_hbm.shape[0]
     width = n_mp * feats
     fy = feats // Y
-    per_class = n_dp // C
+    per_class = ZL // C
     d, m = lax.axis_index("dp"), lax.axis_index("mp")
     z, x = lax.div(d, X), lax.rem(d, X)
     h, y, c = lax.div(m, Y * C), lax.rem(lax.div(m, C), Y), lax.rem(m, C)
@@ -210,8 +234,16 @@
     twin = (d, (h * Y + y) * C + (1 - c))
     other = 1 - c
 
-    load_w = pltpu.make_async_copy(w_hbm, w_ref, w_sem)
-    load_w.start()
+    loads = [
+        pltpu.make_async_copy(src, dst, in_sem.at[i])
+        for i, (src, dst) in enumerate([
+            (owner_hbm, owner_ref), (patches_hbm, patches_ref), (slot_hbm, slot_ref),
+            (gain_hbm, gain_ref), (seg_hbm, seg_ref), (qg_hbm, qg_ref), (kg_hbm, kg_ref),
+            (cot_hbm, cot_ref), (w_hbm, w_ref),
+        ])
+    ]
+    for load in loads:
+        load.start()
 
     barrier = pltpu.get_barrier_semaphore()
 
@@ -225,6 +257,8 @@
     for dev in near:
         pl.semaphore_signal(barrier, inc=1, device_id=dev, device_id_type=MESH)
 
+    for load in loads[:4]:
+        load.wait()
     owners = jnp.broadcast_to(owner_ref[...].astype(F32), (ROWS, ROWS))
     rows_i = lax.broadcasted_iota(jnp.int32, (ROWS, ROWS), 0)
     cols_i = lax.broadcasted_iota(jnp.int32, (ROWS, ROWS), 1)
@@ -282,7 +316,7 @@
             ring_y,
             lambda q: gath.at[(hh * Y + q) * C + c],
             lambda q, i: gath.at[(hh * Y + q) * C + c, pl.ds(i * (feats // 2), feats // 2)],
-            yg_s, yg_r, idx * 4,
+            yg_s, yg_r, idx,
         )
 
     def twin_copy(idx, hh, q, core):
@@ -306,6 +340,7 @@
 
     def next_y(i):
         g_y[i].relay()
+        g_y[i].rest()
         to_twin(i, come[i], near_y)
 
     def last_y(i):
@@ -316,16 +351,20 @@
     own_y(0)
     next_y(0)
     g_h.relay()
-    for i in range(1, min(len(come), 3)):
+    last_y(0)
+    g_h.rest()
+    near_h = range(1, min(len(come), 3))
+    for i in near_h:
         own_y(i)
-    last_y(0)
+    for i in near_h:
+        next_y(i)
+    for i in near_h:
+        last_y(i)
     g_h.last()
     if ZH == 4:
         own_y(3)
-    for i in range(1, len(come)):
-        next_y(i)
-    for i in range(1, len(come)):
-        last_y(i)
+        next_y(3)
+        last_y(3)
     if C == 2:
         for i, hh in enumerate(come):
             for q in range(Y):
@@ -342,7 +381,8 @@
     row_var = jnp.sum(s2, axis=0, keepdims=True) / width - row_mean * row_mean
     inverse = lax.rsqrt(row_var + 1e-06)
 
-    load_w.wait()
+    for load in loads[4:]:
+        load.wait()
     step = 4
 
     def project(j, acc):
@@ -356,55 +396,53 @@
         0, n_mp // step, project, jnp.zeros((ROWS, 3 * HEAD), F32)
     ).astype(BF16)
 
-    mine = lax.rem(c + C * n_dp - d, C)
-
-    def nt_copy(i, to):
+    mine = lax.rem(c + C * ZL - z, C)
+    share = pl.ds(pl.multiple_of(y * fy, fy), fy)
+
+    def nt_copy(i):
+        to = i * C + mine
         return rcopy(
-            nt.at[to, pl.ds(pl.multiple_of(y * fy, fy), fy)],
-            br.at[y, c, lax.div(d, C)],
-            nt_s.at[i], nt_r.at[lax.div(d, C)], (to, m),
+            nt.at[pl.ds(to * X, X), share], br.at[y, c, lax.div(z, C)],
+            nt_s.at[i], nt_r.at[lax.div(z, C)], (to * X + x, m),
         )
 
-    def nt_send(k, _):
-        i = lax.rem(lax.div(d, C) + k, per_class)
-        to = i * C + mine
-
-        @pl.when(to != d)
-        def _():
-            nt_copy(i, to).start()
-
-        return 0
-
-    lax.fori_loop(0, per_class, nt_send, 0)
-
-    @pl.when(mine == lax.rem(d, C))
+    def partners(fn):
+        def one(i, _):
+            @pl.when(i * C + mine != z)
+            def _():
+                fn(i)
+
+            return 0
+
+        lax.fori_loop(0, per_class, one, 0)
+
+    partners(lambda i: nt_copy(i).start())
+
+    @pl.when(mine == lax.rem(z, C))
     def _():
-        br[y, c, lax.div(d, C)] = nt[d, pl.ds(pl.multiple_of(y * fy, fy), fy)]
+        br[y, c, lax.div(z, C)] = nt[pl.ds(z * X, X), share]
 
     seg = jnp.broadcast_to(seg_ref[...].astype(F32), (ROWS, ROWS))
     attended, grads = head_pass(
         projected, qg_ref[...], kg_ref[...], seg == seg.T, cot_ref[...]
     )
-    ga[d] = grads
-
-    def z_copy(level, up):
-        dev = (d + X, m) if up else (d - X, m)
-        ref = ga.at[level * X + x]
-        i = level + (ZL if up else 0)
-        return rcopy(ref, ref, zg_s.at[i], zg_r.at[level], dev)
-
-    def z_wait(level):
-        ref = ga.at[level * X + x]
-        dev = (lax.rem(d + X, n_dp), m)
-        rcopy(ref, ref, zg_s.at[level], zg_r.at[level], dev).wait_recv()
-
-    def gather_x(level):
-        return Gather(
-            ring_x,
-            lambda q: ga.at[level * X + q],
-            lambda q, i: ga.at[level * X + q, pl.ds(i * (ROWS // 2), ROWS // 2)],
-            xg_s, xg_r, level * 4,
-        )
+    ga[z] = grads
+
+    def z_half(level, i):
+        return ga.at[level, pl.ds(i * (ROWS // 2), ROWS // 2)]
+
+    def z_copy(level, up, i, far=False):
+        step = X * EXPRESS if far else X
+        dev = (d + step, m) if up else (d - step, m)
+        at = level * 2 + i
+        ref = z_half(level, i)
+        out = at + (2 * ZL if up else 0) + (4 * ZL if far else 0)
+        return rcopy(ref, ref, zg_s.at[out], zg_r.at[at], dev)
+
+    def z_wait(level, i):
+        ref = z_half(level, i)
+        at = level * 2 + i
+        rcopy(ref, ref, zg_s.at[at], zg_r.at[at], (lax.rem(d + X, n_dp), m)).wait_recv()
 
     def levels(k, fn):
         @pl.when(z >= k)
@@ -415,30 +453,29 @@
         def _():
             fn(z + k, False)
 
-    def z_step(level, below):
-        z_wait(level)
-        if below:
-
-            @pl.when(z < ZL - 1)
-            def _():
-                z_copy(level, True).start()
-        else:
-
-            @pl.when(z > 0)
-            def _():
-                z_copy(level, False).start()
-
-        gather_x(level).send()
-
-    @pl.when(z < ZL - 1)
-    def _():
-        z_copy(z, True).start()
-
-    @pl.when(z > 0)
-    def _():
-        z_copy(z, False).start()
-
-    gather_x(z).send()
+    def z_on(level, below, k, fn):
+        for up in (True, False):
+            if k == 0 or (below == up and k % EXPRESS != EXPRESS - 1):
+
+                @pl.when((z < ZL - 1) if up else (z > 0))
+                def _():
+                    fn(level, up, False)
+
+            if k == 0 and EXPRESS < ZL:
+
+                @pl.when((z + EXPRESS < ZL) if up else (z >= EXPRESS))
+                def _():
+                    fn(level, up, True)
+
+    def z_step(k, i):
+        def one(level, below):
+            z_wait(level, i)
+            z_on(level, below, k, lambda level, up, far: z_copy(level, up, i, far).start())
+
+        return one
+
+    for i in (0, 1):
+        z_on(z, None, 0, lambda level, up, far: z_copy(level, up, i, far).start())
     attn_ref[...] = attended
 
     order = ring_h.others() + [h]
@@ -465,7 +502,7 @@
             lambda q: ts.at[hh, c, q],
             lambda q, i: ts.at[hh, c, q, pl.ds(i * (feats // 2), feats // 2)],
             [ya.at[idx], yb.at[idx], yl.at[idx], yr.at[idx]],
-            yr_s, yr_r, idx * 4,
+            yr_s, yr_r, idx,
         )
 
     s_y = [scatter_y(i) for i in range(len(order))]
@@ -502,16 +539,9 @@
     def n_copy(q, core):
         return rcopy(br.at[q, core], br.at[q, core], nc_s.at[q], nc_r.at[q], twin)
 
-    def n_wait(k, _):
-        i = lax.rem(lax.div(d, C) + per_class - k, per_class)
-
-        @pl.when(i * C + mine != d)
-        def _():
-            rcopy(
-                br.at[y, c, i], br.at[y, c, i], nt_s.at[i], nt_r.at[i], (lax.rem(d + 1, n_dp), m)
-            ).wait_recv()
-
-        return 0
+    def n_wait(i):
+        ref = br.at[y, c, i]
+        rcopy(ref, ref, nt_s.at[i], nt_r.at[i], (lax.rem(d + X, n_dp), m)).wait_recv()
 
     def n_to_twin(qs):
         if C == 2:
@@ -519,12 +549,13 @@
                 n_copy(q, c).start()
 
     def n_first():
-        lax.fori_loop(0, per_class, n_wait, 0)
+        partners(n_wait)
         g_n.send()
         n_to_twin([y])
 
     def n_second():
         g_n.relay()
+        g_n.rest()
         n_to_twin(near_y)
 
     def n_third():
@@ -539,50 +570,53 @@
     every = range(len(order))
     jobs = [
         [functools.partial(rs_a, i) for i in every] + [n_first],
-        [functools.partial(rs_b, i) for i in every],
-        [functools.partial(rs_c, i) for i in every] + [s_h.first, n_second],
-        [s_h.second, n_third],
+        [functools.partial(rs_b, i) for i in every] + [n_second],
+        [functools.partial(rs_c, i) for i in every] + [s_h.first, n_third],
         [n_last],
+        [],
+        [],
+        [s_h.second],
     ]
-    jobs = jobs + [[]] * (ZL - 1 - len(jobs))
-    span = max(ZL - 1, 1)
-    for k in range(1, ZL):
-        levels(k, z_step)
-        share = jobs[(k - 1) * len(jobs) // span : k * len(jobs) // span]
-        for group in share:
-            for job in group:
-                job()
-        if k == 1:
-            gather_x(z).relay()
-        else:
-            levels(k - 1, lambda level, _: gather_x(level).relay())
-    if ZL == 1:
-        for group in jobs:
-            for job in group:
-                job()
-        gather_x(z).relay()
-    else:
-        levels(ZL - 1, lambda level, _: gather_x(level).relay())
-
-    wg_ref[...] = jnp.zeros_like(wg_ref)
-
-    def weight_term(level):
-        gather_x(level).last()
-        left = []
-        for q in range(X):
-            src = level * X + q
-            kind = lax.rem(d + src, C)
-            left.append(br[:, kind, lax.div(src, C)].reshape(feats, ROWS))
-        right = ga[pl.ds(level * X, X)].reshape(X * ROWS, 3 * HEAD)
-        wg_ref[...] += dot(jnp.concatenate(left, axis=1), right, 1, 0)
-
-    weight_term(z)
-
-    def weight_step(k, _):
-        levels(k, lambda level, _: weight_term(level))
-        return 0
-
-    lax.fori_loop(1, ZL, weight_step, 0)
+
+    def weight_term(level, _=None):
+        kind, i = lax.rem(z + level, C), lax.div(level, C)
+        left = [br[:, kind, i, q].reshape(feats, ROWS) for q in range(X)]
+        wa[...] += dot(jnp.concatenate(left, axis=0), ga[level], 1, 0)
+
+    away = sorted(range(1, ZL), key=lambda k: (k // EXPRESS + k % EXPRESS, k))
+
+    def weight_terms(first, last):
+        def one(at, _):
+            k = at + 1
+            for i, value in enumerate(away):
+                k = jnp.where(at == i, value, k)
+            levels(k, weight_term)
+            return 0
+
+        lax.fori_loop(first, last, one, 0)
+
+    wa[...] = jnp.zeros_like(wa)
+    for at in range(max(len(away), len(jobs))):
+        if at < len(away):
+            levels(away[at], z_step(away[at], 0))
+            levels(away[at], z_step(away[at], 1))
+        for job in jobs[at] if at < len(jobs) else []:
+            job()
+        if at == 4:
+            weight_term(z)
+            weight_terms(0, min(at, len(away)))
+    weight_terms(min(4, len(away)), len(away))
+    wb[...] = wa[...].astype(BF16).reshape(wb.shape)
+    s_x = Scatter(
+        ring_x,
+        lambda q: wb.at[q],
+        lambda q, i: wb.at[q, pl.ds(i * (feats // 2), feats // 2)],
+        [xa, xb, xl, xr],
+        xs_s, xs_r, 0,
+    )
+    s_x.first()
+    s_x.second()
+    wg_ref[...] = s_x.total()
     ng_ref[...] = s_h.total()
 
     def a2a_drain(k, _):
@@ -599,14 +633,7 @@
             for q in range(Y):
                 twin_copy(i, hh, q, c).wait_send()
 
-    def nt_drain(i, _):
-        @pl.when(i * C + mine != d)
-        def _():
-            nt_copy(i, i * C + mine).wait_send()
-
-        return 0
-
-    lax.fori_loop(0, per_class, nt_drain, 0)
+    partners(lambda i: nt_copy(i).wait_send())
     g_n.drain()
     if C == 2:
         for q in range(Y):
@@ -617,28 +644,14 @@
         s_y[i].drain()
     s_h.drain()
 
-    @pl.when(z < ZL - 1)
-    def _():
-        z_copy(z, True).wait_send()
-
-    @pl.when(z > 0)
-    def _():
-        z_copy(z, False).wait_send()
-
-    gather_x(z).drain()
-
-    def far_drain(level, below):
-        @pl.when((z < ZL - 1) if below else (z > 0))
-        def _():
-            z_copy(level, below).wait_send()
-
-        gather_x(level).drain()
-
-    def z_drain(k, _):
-        levels(k, far_drain)
-        return 0
-
-    lax.fori_loop(1, ZL, z_drain, 0)
+    def z_sent(level, up, far):
+        for i in (0, 1):
+            z_copy(level, up, i, far).wait_send()
+
+    z_on(z, None, 0, z_sent)
+    for k in away:
+        levels(k, lambda level, below: z_on(level, below, k, z_sent))
+    s_x.drain()
 
 
 def on_device(
@@ -652,11 +665,22 @@
     dma = lambda n: pltpu.SemaphoreType.DMA((max(n, 1),))
     half = feats // 2
     pairs = []
-    for n in (n_dp, 4, 4 * ZH, ZH * Y, n_dp // C, 4, Y):
+    for n in (n_dp, 6, 6 * ZH, ZH * Y, ZL // C, 6, Y):
         pairs += [dma(n), dma(n)]
-    pairs += [dma(2 * ZL), dma(ZL), dma(4 * ZL), dma(4 * ZL)]
-    for n in (ZH, 4 * ZH, 4):
+    pairs += [dma(8 * ZL), dma(2 * ZL), dma(6), dma(6)]
+    for n in (ZH, 6 * ZH, 6):
         pairs += [dma(n), dma(n)]
+    operands = (
+        patches.T,
+        route_owner.reshape(1, ROWS),
+        route_slot.reshape(1, ROWS),
+        segment_ids,
+        ln_gain.reshape(width // 128, 128),
+        qkv_weight,
+        q_gain.reshape(1, HEAD),
+        k_gain.reshape(1, HEAD),
+        d_attn,
+    )
     return pl.pallas_call(
         kernel,
         out_shape=(
@@ -664,18 +688,18 @@
             jax.ShapeDtypeStruct((feats, ROWS), F32),
             jax.ShapeDtypeStruct((width // n_dp, 3 * HEAD), F32),
         ),
-        in_specs=[vmem] * 5 + [pl.BlockSpec(memory_space=pl.ANY)] + [vmem] * 3,
+        in_specs=[pl.BlockSpec(memory_space=pl.ANY)] * 9,
         out_specs=(vmem, vmem, vmem),
         scratch_shapes=[
-            pltpu.VMEM((width, 3 * HEAD), BF16),
+            *[pltpu.VMEM(a.shape, a.dtype) for a in operands],
             pltpu.VMEM((width, 128), F32),
             pltpu.VMEM((ext, ROWS), BF16),
             pltpu.VMEM((n_dp, SLOT, ext), BF16),
             pltpu.VMEM((n_dp, SLOT, ext), BF16),
             pltpu.VMEM((n_mp, feats, ROWS), BF16),
             pltpu.VMEM((n_mp, feats, ROWS), BF16),
-            pltpu.VMEM((Y, C, n_dp // C, feats // Y, ROWS), BF16),
-            pltpu.VMEM((n_dp, ROWS, 3 * HEAD), BF16),
+            pltpu.VMEM((Y, C, ZL // C, X, feats // Y, ROWS), BF16),
+            pltpu.VMEM((ZL, ROWS, 3 * HEAD), BF16),
             pltpu.VMEM((ZH, C, Y, feats, ROWS), BF16),
             pltpu.VMEM((ZH, Y, feats, ROWS), BF16),
             pltpu.VMEM((ZH, half, ROWS), BF16),
@@ -687,23 +711,19 @@
             pltpu.VMEM((half, ROWS), BF16),
             pltpu.VMEM((feats, ROWS), BF16),
             pltpu.VMEM((feats, ROWS), BF16),
-            pltpu.SemaphoreType.DMA,
+            pltpu.VMEM((X * feats, 3 * HEAD), F32),
+            pltpu.VMEM((X, feats, 3 * HEAD), BF16),
+            pltpu.VMEM((half, 3 * HEAD), BF16),
+            pltpu.VMEM((half, 3 * HEAD), BF16),
+            pltpu.VMEM((feats, 3 * HEAD), BF16),
+            pltpu.VMEM((feats, 3 * HEAD), BF16),
+            dma(len(operands)),
             *pairs,
         ],
         compiler_params=pltpu.CompilerParams(
-            collective_id=0, has_side_effects=True, vmem_limit_bytes=48 * 1024 * 1024
+            collective_id=0, has_side_effects=True, vmem_limit_bytes=62 * 1024 * 1024
         ),
-    )(
-        patches.T,
-        route_owner.reshape(1, ROWS),
-        route_slot.reshape(1, ROWS),
-        segment_ids,
-        ln_gain.reshape(width // 128, 128),
-        qkv_weight,
-        q_gain.reshape(1, HEAD),
-        k_gain.reshape(1, HEAD),
-        d_attn,
-    )
+    )(*operands)
 
 
 def solution(mesh):

time: 140 us -> 130 us (0.929)
  local copies, waits for them, and re-layouts: 9.87 us -> 4.61 us
  Pallas kernels: 127 us -> 123 us
    unnamed x21 -> x3, local copies, waits for them, and re-layouts: 9.87 us -> 4.61 us
    pallas_call x1, Pallas kernels: 127 us -> 123 us  [on_device(): pl.pallas_call(kernel, out_shape=(jax.ShapeDtypeStruct((ROWS, HEAD), BF16...]
where the time goes in v2:
time: 130 us; the launch traced here: 128 us
  Pallas kernels  123 us (95%)
  local copies, waits for them, and re-layouts  4.61 us (4%)
    pallas_call x1, Pallas kernels, on_device(): pl.pallas_call(kernel, out_shape=(jax.ShapeDtypeStruct((ROWS, HEAD), BF16...  123 us
    unnamed x3, local copies, waits for them, and re-layouts  4.61 us

profile of v2, /device:TPU:24, one launch (start us, length us, event | category | flops | bytes accessed | tf_op | source)
XLA Modules:
  0.0 127.9 jit_solution(1401804038502308355)
XLA Ops:
  0.6 122.7 %shard_map.112 = (bf16[128,128]{1,0:T(8,128)(2,1)}, f32[192,128]{1,0:T(8,128)}, f32[192,384]{1,0:T(8,128)}) custom-call(bf16[192,128]{1,0:T(8,128)(2,1)} %bitcast.6, s32[1,128]{1,0:T(1,128)} %bitcast.8, s32[1,128]{1,0:T(1,128)} %bitcast.9, s32[1,128]{1,0:T(1,128)} %seg_hbm.1, f32[48,128]{1,0:T(8,128)} %bitcast.7, bf16[6144,384]{1,0:T(8,128)(2,1)} %w_hbm.1, ...), custom_call_target="tpu_custom_call" | custom-call | tf_op jit(solution)/shard_map/pallas_call | solution.py:684
  123.3 1.4 %copy.15 = bf16[128,128]{1,0:T(8,128)(2,1)} copy(bf16[128,128]{1,0:T(8,128)(2,1)} %get-tuple-element.6) | data formatting | bytes 65536
  124.7 1.5 %copy.16 = f32[192,128]{1,0:T(8,128)} copy(f32[192,128]{1,0:T(8,128)} %get-tuple-element.7) | data formatting | bytes 196608
  126.2 1.7 %copy.17 = f32[192,384]{1,0:T(8,128)} copy(f32[192,384]{1,0:T(8,128)} %get-tuple-element.8) | data formatting | bytes 589824

commit v3 on v2

--- a/solution.py
+++ b/solution.py
@@ -652,6 +652,12 @@
     for k in away:
         levels(k, lambda level, below: z_on(level, below, k, z_sent))
     s_x.drain()
+
+
+def deliver(a_ref, b_ref, c_ref, a_out, b_out, c_out):
+    a_out[...] = a_ref[...]
+    b_out[...] = b_ref[...]
+    c_out[...] = c_ref[...]
 
 
 def on_device(
@@ -681,14 +687,16 @@
         k_gain.reshape(1, HEAD),
         d_attn,
     )
-    return pl.pallas_call(
+    out_shape = (
+        jax.ShapeDtypeStruct((ROWS, HEAD), BF16),
+        jax.ShapeDtypeStruct((feats, ROWS), F32),
+        jax.ShapeDtypeStruct((width // n_dp, 3 * HEAD), F32),
+    )
+    anywhere = pl.BlockSpec(memory_space=pl.ANY)
+    results = pl.pallas_call(
         kernel,
-        out_shape=(
-            jax.ShapeDtypeStruct((ROWS, HEAD), BF16),
-            jax.ShapeDtypeStruct((feats, ROWS), F32),
-            jax.ShapeDtypeStruct((width // n_dp, 3 * HEAD), F32),
-        ),
-        in_specs=[pl.BlockSpec(memory_space=pl.ANY)] * 9,
+        out_shape=out_shape,
+        in_specs=[anywhere] * 9,
         out_specs=(vmem, vmem, vmem),
         scratch_shapes=[
             *[pltpu.VMEM(a.shape, a.dtype) for a in operands],
@@ -724,6 +732,13 @@
             collective_id=0, has_side_effects=True, vmem_limit_bytes=62 * 1024 * 1024
         ),
     )(*operands)
+    return pl.pallas_call(
+        deliver,
+        out_shape=out_shape,
+        in_specs=[vmem] * 3,
+        out_specs=(vmem,) * 3,
+        compiler_params=pltpu.CompilerParams(vmem_limit_bytes=62 * 1024 * 1024),
+    )(*results)
 
 
 def solution(mesh):

time: 130 us -> 128 us (0.985)
  local copies, waits for them, and re-layouts: 4.61 us -> 0 us
    unnamed x3 -> x0, local copies, waits for them, and re-layouts: 4.61 us -> none
    pallas_call x1 -> x2, Pallas kernels: 123 us -> 124 us  [the longest x1 123 us: on_device(): pl.pallas_call(kernel, out_shape=out_shape, in_specs=[anywhere] * 9, out_...]
where the time goes in v3:
time: 128 us; the launch traced here: 125 us
  Pallas kernels  124 us (97%)
    pallas_call x1, Pallas kernels, on_device(): pl.pallas_call(kernel, out_shape=out_shape, in_specs=[anywhere] * 9, out_...  123 us

profile of v3, /device:TPU:24, one launch (start us, length us, event | category | flops | bytes accessed | tf_op | source)
XLA Modules:
  0.0 125.1 jit_solution(8896813321678133278)
XLA Ops:
  0.6 122.7 %shard_map.112 = (bf16[128,128]{1,0:T(8,128)(2,1)}, f32[192,128]{1,0:T(8,128)}, f32[192,384]{1,0:T(8,128)}) custom-call(bf16[192,128]{1,0:T(8,128)(2,1)} %bitcast.6, s32[1,128]{1,0:T(1,128)} %bitcast.8, s32[1,128]{1,0:T(1,128)} %bitcast.9, s32[1,128]{1,0:T(1,128)} %seg_hbm.1, f32[48,128]{1,0:T(8,128)} %bitcast.7, bf16[6144,384]{1,0:T(8,128)(2,1)} %w_hbm.1, ...), custom_call_target="tpu_custom_call" | custom-call | tf_op jit(solution)/shard_map/pallas_call | solution.py:696
  123.3 1.8 %shard_map.113 = (bf16[128,128]{1,0:T(8,128)(2,1)}, f32[192,128]{1,0:T(8,128)}, f32[192,384]{1,0:T(8,128)}) custom-call(bf16[128,128]{1,0:T(8,128)(2,1)} %get-tuple-element.6.a_ref, f32[192,128]{1,0:T(8,128)} %get-tuple-element.7.b_ref, f32[192,384]{1,0:T(8,128)} %get-tuple-element.8.c_ref), custom_call_target="tpu_custom_call" | custom-call | tf_op jit(solution)/shard_map/pallas_call | solution.py:735

commit v4 on v3

--- a/solution.py
+++ b/solution.py
@@ -615,10 +615,6 @@
         xs_s, xs_r, 0,
     )
     s_x.first()
-    s_x.second()
-    wg_ref[...] = s_x.total()
-    ng_ref[...] = s_h.total()
-
     def a2a_drain(k, _):
         to = lax.rem(d + k, n_dp)
         rcopy(out_buf.at[to], arr.at[d], a2a_s.at[to], a2a_r.at[d], (to, m)).wait_send()
@@ -642,6 +638,10 @@
             core_copy(i).wait_send()
     for i in every:
         s_y[i].drain()
+    s_x.second()
+    wg_ref[...] = s_x.total()
+    ng_ref[...] = s_h.total()
+
     s_h.drain()
 
     def z_sent(level, up, far):

time: 128 us -> 127 us (level)
  no operation moved by 1% of the time
where the time goes in v4:
time: 127 us; the launch traced here: 125 us
  Pallas kernels  124 us (98%)
    pallas_call x1, Pallas kernels, on_device(): pl.pallas_call(kernel, out_shape=out_shape, in_specs=[anywhere] * 9, out_...  122 us

profile of v4, /device:TPU:24, one launch (start us, length us, event | category | flops | bytes accessed | tf_op | source)
XLA Modules:
  0.0 124.6 jit_solution(9161423230241162494)
XLA Ops:
  0.6 122.1 %shard_map.112 = (bf16[128,128]{1,0:T(8,128)(2,1)}, f32[192,128]{1,0:T(8,128)}, f32[192,384]{1,0:T(8,128)}) custom-call(bf16[192,128]{1,0:T(8,128)(2,1)} %bitcast.6, s32[1,128]{1,0:T(1,128)} %bitcast.8, s32[1,128]{1,0:T(1,128)} %bitcast.9, s32[1,128]{1,0:T(1,128)} %seg_hbm.1, f32[48,128]{1,0:T(8,128)} %bitcast.7, bf16[6144,384]{1,0:T(8,128)(2,1)} %w_hbm.1, ...), custom_call_target="tpu_custom_call" | custom-call | tf_op jit(solution)/shard_map/pallas_call | solution.py:696
  122.8 1.8 %shard_map.113 = (bf16[128,128]{1,0:T(8,128)(2,1)}, f32[192,128]{1,0:T(8,128)}, f32[192,384]{1,0:T(8,128)}) custom-call(bf16[128,128]{1,0:T(8,128)(2,1)} %get-tuple-element.6.a_ref, f32[192,128]{1,0:T(8,128)} %get-tuple-element.7.b_ref, f32[192,384]{1,0:T(8,128)} %get-tuple-element.8.c_ref), custom_call_target="tpu_custom_call" | custom-call | tf_op jit(solution)/shard_map/pallas_call | solution.py:735
